TPU v7x, 1024 devices: a whole 4x8x16 slice. The times are simulated.
1024 devices in a mesh: island: 16 (over y, core), ep: 16 (over z), tp: 4 (over x).
Axes of the slice: x: 4, y: 8, z: 16, core: 2. Of those that a mesh axis runs over, the one named last changes fastest.
Arguments:
- tokens: bfloat16 [32768, 2048], P(('island', 'ep')), may hold values from -6 to 6
- cotangent: bfloat16 [32768, 2048], P(('island', 'ep')), may hold values from -6 to 6
- expert_ids: int32 [32768, 1], P(('island', 'ep')), may hold values from 0 to 15; in each aligned block of 128 rows (0 to 127, 128 to 255, ...) at most 10 rows name the same one
- gate_probs: float32 [32768, 1], P(('island', 'ep')), may hold values from 0.1 to 1
- w_gate: bfloat16 [16, 2048, 768], P('ep', None, 'tp'), may hold values from -0.125 to 0.125
- w_up: bfloat16 [16, 2048, 768], P('ep', None, 'tp'), may hold values from -0.125 to 0.125
- w_down: bfloat16 [16, 768, 2048], P('ep', 'tp'), may hold values from -0.21875 to 0.21875
Outputs:
- token_grad: bfloat16 [32768, 2048], P(('island', 'ep'), 'tp')
- prob_grad: float32 [32768, 1], P(('island', 'ep'))
- grad_gate: float32 [16, 2048, 768], P('ep', 'island', 'tp')
- grad_up: float32 [16, 2048, 768], P('ep', 'island', 'tp')
- grad_down: float32 [16, 768, 2048], P('ep', 'tp', 'island')
Inputs may be any that keep to these rules, and one draw needn't show every extreme that they name: `expert_ids`: each row names one expert; in each aligned block of 128 rows (one index of island and ep) no expert is named by more than 10 rows, a bound that some block reaches.
All inputs are finite; a program needn't handle non-finite values.
Results may differ from a plain program's by a relative error of at most 0.025.
Values may be sent and summed in bfloat16 or wider, within the bound.
A program may use at most 32 MiB of HBM per device.

v0:
```python
import functools

import jax
import jax.numpy as jnp
from jax import lax
from jax.experimental import pallas as pl
from jax.experimental.pallas import tpu as pltpu
from jax.sharding import PartitionSpec as P

CAP = 10
ROWS = 16
SPARE = ROWS - CAP
LANES = 128
TAIL = 4 * LANES
BF = jnp.bfloat16
F32 = jnp.float32
MESH = pl.DeviceIdType.MESH
NT = ((1,), (1,))


def dot(a, b, dims=((1,), (0,)), precision=None):
    return lax.dot_general(
        a, b, (dims, ((), ())), preferred_element_type=F32, precision=precision
    )


def iota(shape, dim):
    return lax.broadcasted_iota(jnp.int32, shape, dim)


def hot(condition):
    return jnp.where(condition, 1.0, 0.0).astype(BF)


def hops(nz):
    near = [1, 2] if nz > 8 else []
    pairs = []
    for d in range(nz // 2 - 1, len(near), -1):
        pairs += [d] + near[len(pairs) // 2 : len(pairs) // 2 + 1]
    return [nz // 2] + [d for pair in pairs for d in (pair, nz - pair)]


def kernel(
    nz, ny,
    tok, cot, ids_ref, probs_ref, wg, wu, wd,
    tg_ref, pg_ref, gg_ref, gu_ref, gd_ref,
    w, tq, cq, sb, rb, xs, ds, mx, md, gt, mgt, ch, cs, yl, yr, ip, xq, pk, rs, rr,
    ld, zs, zr, fs, fr, ms, mr, ps, pr, hs, hr, ys, yrs, vs, vr,
):
    t, z, island = lax.axis_index("tp"), lax.axis_index("ep"), lax.axis_index("island")
    y = lax.div(island, 2)
    core = island - 2 * y
    toks, quarter = tq.shape
    ff = wg.shape[0]
    m = nz * CAP
    n = nz * ROWS
    half = m // 2
    band = xs.shape[3]
    pairs = xs.shape[0]
    hz, hy = nz // 2, ny // 2
    piece_rows = 3 * ff // 4

    def tp_at(r):
        return {"tp": lax.rem(t + r, 4)}

    def ep_at(d):
        return {"ep": lax.rem(z + d, nz)}

    def y_at(d):
        return {"island": 2 * lax.rem(y + d, ny) + core}

    mate = {"island": 2 * y + 1 - core}

    def remote(src, dst, ssem, rsem, device):
        return pltpu.make_async_remote_copy(
            src_ref=src, dst_ref=dst, send_sem=ssem, recv_sem=rsem,
            device_id=device, device_id_type=MESH,
        )

    loads = [
        pltpu.make_async_copy(tok.at[:, pl.ds(pl.multiple_of(t * quarter, quarter), quarter)], tq, ld.at[0]),
        pltpu.make_async_copy(cot.at[:, pl.ds(pl.multiple_of(t * quarter, quarter), quarter)], cq, ld.at[1]),
        pltpu.make_async_copy(wg, w.at[pl.ds(0, ff)], ld.at[2]),
        pltpu.make_async_copy(wu, w.at[pl.ds(ff, ff)], ld.at[3]),
        pltpu.make_async_copy(wd, w.at[pl.ds(2 * ff, ff)], ld.at[4]),
    ]
    for copy in loads:
        copy.start()

    barrier = pltpu.get_barrier_semaphore()
    peers = [ep_at(d) for d in range(1, nz)] + [tp_at(r) for r in (1, 2, 3)]
    peers += [y_at(1), y_at(ny - 1), mate]
    for peer in peers:
        pl.semaphore_signal(barrier, inc=1, device_id=peer, device_id_type=MESH)

    ids = ids_ref[...]
    probs = probs_ref[...]
    named = hot(iota((nz, toks), 0) == ids)
    earlier = hot(iota((toks, toks), 0) < iota((toks, toks), 1))
    rank = jnp.sum(named.astype(F32) * dot(named, earlier), 0, keepdims=True)
    eye = iota((toks, toks), 0) == iota((toks, toks), 1)

    def column(row):
        return jnp.sum(jnp.where(eye, row, 0.0), 1, keepdims=True)

    probs_col = column(probs)
    ids_col = column(ids.astype(F32)).astype(jnp.int32)
    rank_col = column(rank).astype(jnp.int32)
    rank = rank.astype(jnp.int32)

    place = iota((n, toks), 0)
    block, row = lax.shift_right_logical(place, 4), place & (ROWS - 1)
    mine = block == ids
    pick_x = hot(mine & (row == rank))
    pick_d = hot(mine & (row == rank + CAP))
    piece = lax.shift_right_logical(row, 2)
    late = mine & ((row & 3) + SPARE == rank)
    pick_tail = [hot(late & (piece == c)) for c in range(4)]

    loads[0].wait()
    loads[1].wait()
    own_x = tq[...]
    own_d = (cq[...].astype(F32) * probs_col).astype(BF)
    main = dot(jnp.concatenate([pick_x, pick_d], 1), jnp.concatenate([own_x, own_d], 0))
    tail = dot(
        jnp.concatenate(pick_tail, 1),
        jnp.concatenate([own_d[:, LANES * c : LANES * (c + 1)] for c in range(4)], 0),
    )
    sb[:, :, 0:quarter] = main.astype(BF).reshape(nz, ROWS, quarter)
    sb[:, :, quarter : quarter + LANES] = tail.astype(BF).reshape(nz, ROWS, LANES)

    pl.semaphore_wait(barrier, len(peers))

    order = hops(nz)

    def z_copy(k):
        d = order[k]
        return remote(sb.at[lax.rem(z + d, nz)], rb.at[t, k + 1], zs.at[k], zr.at[k], ep_at(d))

    z_copies = [z_copy(k) for k in range(nz - 1)]
    own_block = pltpu.make_async_copy(sb.at[z], rb.at[t, 0], ld.at[5])
    own_block.start()
    for copy in z_copies:
        copy.start()

    left_q, right_q, far_q = lax.rem(t + 3, 4), lax.rem(t + 1, 4), lax.rem(t + 2, 4)

    def pass_right(p):
        return remote(rb.at[t, p], rb.at[t, p], fs.at[0, p], fr.at[0, p], tp_at(1))

    def pass_left(p):
        return remote(rb.at[t, p], rb.at[t, p], fs.at[1, p], fr.at[1, p], tp_at(3))

    def from_left(p):
        return remote(rb.at[t, p], rb.at[left_q, p], fs.at[0, p], fr.at[0, p], tp_at(1))

    def from_right(p):
        return remote(rb.at[t, p], rb.at[right_q, p], fs.at[1, p], fr.at[1, p], tp_at(3))

    direct = nz - 4 if nz > 8 else nz // 2

    def onward(p):
        if p >= direct:
            return remote(rb.at[t, p], rb.at[t, p], fs.at[2, p], fr.at[2, p], tp_at(2))
        q, to = (right_q, 3) if p % 2 else (left_q, 1)
        return remote(rb.at[q, p], rb.at[q, p], fs.at[2, p], fr.at[2, p], tp_at(to))

    def from_far(p):
        return remote(rb.at[t, p], rb.at[far_q, p], fs.at[2, p], fr.at[2, p], tp_at(1))

    def relay(p):
        from_left(p).wait_recv()
        from_right(p).wait_recv()
        onward(p).start()

    behind = 4
    for p in range(nz):
        if p == 0:
            own_block.wait()
        else:
            z_copies[p - 1].wait_recv()
        if p >= direct:
            onward(p).start()
        pass_right(p).start()
        pass_left(p).start()
        if 0 <= p - behind < direct:
            relay(p - behind)
    for p in range(max(0, nz - behind), direct):
        relay(p)

    rows = iota((half, n // 2), 0)
    source = lax.shift_right_logical(rows * 6554, 16)
    slot = rows - CAP * source
    there = iota((half, n // 2), 1)
    unpick_x = hot(there == ROWS * source + slot)
    unpick_d = hot((slot < SPARE) & (there == ROWS * source + CAP + slot))
    unpick_tail = [
        hot((slot >= SPARE) & (there == ROWS * source + 4 * c + slot - SPARE)) for c in range(4)
    ]
    unpick_main = jnp.concatenate([unpick_x, unpick_d], 0)
    unpick_tail = jnp.concatenate(unpick_tail, 0)
    per = quarter // band
    for g in range(2):
        for p in range(g * hz, g * hz + hz):
            if p >= direct:
                from_left(p).wait_recv()
                from_right(p).wait_recv()
            from_far(p).wait_recv()
        here = pl.ds(g * half, half)
        for q in range(4):
            got = rb[q, pl.ds(g * hz, hz)].reshape(n // 2, quarter + LANES)
            both = dot(unpick_main, got[:, 0:quarter])
            ends = dot(unpick_tail, got[:, quarter : quarter + LANES])
            ends = jnp.concatenate([ends[half * c : half * (c + 1)] for c in range(4)], 1)
            x_rows = both[0:half].astype(BF)
            d_rows = (both[half : 2 * half] + ends).astype(BF)
            for b in range(per):
                at = q * per + b
                xs[at // 2, at % 2, here, :] = x_rows[:, band * b : band * (b + 1)]
                ds[at // 2, at % 2, here, :] = d_rows[:, band * b : band * (b + 1)]

    mate_x = remote(xs.at[:, 1 - core], mx, ms.at[0], mr.at[0], mate)
    mate_d = remote(ds.at[:, 1 - core], md, ms.at[1], mr.at[1], mate)
    mate_g = remote(gt, mgt, ms.at[2], mr.at[2], mate)
    mate_x.start()
    mate_d.start()

    for copy in loads[2:]:
        copy.wait()
    x_all = jnp.concatenate([xs[o, c] for o in range(pairs) for c in range(2)], 1)
    d_all = jnp.concatenate([ds[o, c] for o in range(pairs) for c in range(2)], 1)
    gate_up = dot(w[0 : 2 * ff, :], x_all, NT)
    back = dot(w[2 * ff : 3 * ff, :], d_all, NT)
    gate, up = gate_up[0:ff], gate_up[ff : 2 * ff]
    sigma = jax.nn.sigmoid(gate)
    active = gate * sigma
    hidden = (active * up).astype(BF)
    gt[0:ff, :] = (back * up * sigma * (1.0 + gate * (1.0 - sigma))).astype(BF)
    gt[ff : 2 * ff, :] = (back * active).astype(BF)
    gt[2 * ff : 3 * ff, :] = hidden
    mate_g.start()

    eye_m = hot(iota((m, m), 0) == iota((m, m), 1))
    d_rows = dot(eye_m, gt[0 : 2 * ff, :], NT).astype(BF)

    def input_part(r):
        q = lax.rem(t + r, 4)
        cols = pl.ds(pl.multiple_of(q * quarter, quarter), quarter)
        ip[r] = dot(d_rows, w[0 : 2 * ff, cols]).astype(BF)

    def tp_copy(g, r):
        here = pl.ds(g * half, half)
        return remote(ip.at[r, here], xq.at[r - 1, here], hs.at[g, r], hr.at[g, r], tp_at(r))

    tp_copies = [[tp_copy(g, r) for r in (1, 2, 3)] for g in range(2)]

    def weight_part(*js):
        def cat(blocks):
            return blocks[0] if len(blocks) == 1 else jnp.concatenate(blocks, 1)

        os = [lax.rem(y + j, ny) for j in js]
        top = dot(gt[0 : 2 * ff, :], cat([xs[o, core] for o in os]))
        top = top + dot(mgt[0 : 2 * ff, :], cat([mx[o] for o in os]))
        low = dot(gt[2 * ff : 3 * ff, :], cat([ds[o, core] for o in os]))
        low = low + dot(mgt[2 * ff : 3 * ff, :], cat([md[o] for o in os]))
        for i, j in enumerate(js):
            ch[j, 0 : 2 * ff, :] = top[:, band * i : band * (i + 1)]
            ch[j, 2 * ff : 3 * ff, :] = low[:, band * i : band * (i + 1)]

    def y_copy(side, dist, part):
        j = dist if side == 0 else ny - dist
        where = pl.ds(part * piece_rows, piece_rows)
        into = (yl, yr)[side]
        return remote(
            cs.at[j, where], into.at[dist - 1, where],
            ys.at[side, dist, part], yrs.at[side, dist, part], y_at(1 if side == 0 else ny - 1),
        )

    far_parts, near_parts = ((0, 1), (2, 3)), ((2, 3), (0, 1))

    def y_step(side, dist, part):
        j = dist if side == 0 else ny - dist
        where = pl.ds(part * piece_rows, piece_rows)
        if dist == hy or (dist == hy - 1 and part in near_parts[side]):
            cs[j, where, :] = ch[j, where, :].astype(BF)
        else:
            y_copy(side, dist + 1, part).wait_recv()
            came = (yl, yr)[side][dist, where, :].astype(F32)
            cs[j, where, :] = (ch[j, where, :] + came).astype(BF)
        y_copy(side, dist, part).start()

    def y_steps(dist, parts):
        for i in range(2):
            for side in (0, 1):
                y_step(side, dist, parts[side][i])

    for r in (2, 1, 3):
        input_part(r)
        tp_copies[0][r - 1].start()
    for r in (2, 1, 3):
        tp_copies[1][r - 1].start()

    mate_x.wait_recv()
    mate_d.wait_recv()
    mate_g.wait_recv()
    weight_part(hy)
    y_steps(hy, far_parts)
    weight_part(hy - 1, ny - hy + 1)
    y_steps(hy - 1, near_parts)

    prob_row = jnp.sum(hidden.astype(F32) * back, 0, keepdims=True)
    in_source = iota((nz, m), 0) == lax.shift_right_logical(iota((nz, m), 1) * 6554, 16)
    at_row = iota((m, LANES), 0)
    at_slot = iota((m, LANES), 1) == at_row - CAP * lax.shift_right_logical(at_row * 6554, 16)
    pk[0] = dot(
        jnp.where(in_source, prob_row, 0.0), jnp.where(at_slot, 1.0, 0.0),
        precision=lax.Precision.HIGHEST,
    )
    prob_sends = [remote(pk.at[0], pk.at[r], ps.at[r], pr.at[r], tp_at(r)) for r in (1, 2, 3)]
    for copy in prob_sends:
        copy.start()
    input_part(0)
    y_steps(hy - 1, far_parts)
    for dist in range(hy - 2, 0, -1):
        weight_part(dist, ny - dist)

    for copy in prob_sends:
        copy.wait_recv()
    prob = (pk[0] + pk[1]) + (pk[2] + pk[3])
    prob_high = prob.astype(BF)
    prob_low = (prob - prob_high.astype(F32)).astype(BF)
    to = iota((n // 2, half), 0)
    block, row = lax.shift_right_logical(to, 4), to & (ROWS - 1)
    first = CAP * block
    frm = iota((n // 2, half), 1)
    pack = hot((row < CAP) & (frm == first + row))
    pack_0 = hot((row >= CAP) & (frm == first + row - CAP))
    pack_1 = hot((row >= CAP) & (row < ROWS - 2) & (frm == first + row - CAP + SPARE))
    to = iota((n // 2, nz), 0)
    block, row = lax.shift_right_logical(to, 4), to & (ROWS - 1)

    def back_copy(k):
        d = nz - order[k]
        return remote(rs.at[k + 1], rr.at[z], vs.at[k], vr.at[k], ep_at(d))

    def back_recv(k):
        return remote(rs.at[0], rr.at[lax.rem(z + order[k], nz)], vs.at[k], vr.at[k], ep_at(1))

    def send_back(g):
        for copy in tp_copies[g]:
            copy.wait_recv()
        here = pl.ds(g * half, half)
        summed = ip[0, here, :].astype(F32) + xq[0, here, :].astype(F32)
        summed = summed + (xq[1, here, :].astype(F32) + xq[2, here, :].astype(F32))
        summed = summed.astype(BF)
        ends = summed[:, 3 * LANES : 4 * LANES]
        same = block + g * hz == iota((n // 2, nz), 1)
        extra = dot(hot(same & (row == CAP)), prob_high) + dot(hot(same & (row == CAP + 1)), prob_low)
        packed = dot(pack, summed[:, 0 : 3 * LANES])
        packed = packed + jnp.concatenate([dot(pack_0, ends), dot(pack_1, ends), extra], 1)
        rs[pl.ds(g * hz, hz)] = packed.astype(BF).reshape(hz, ROWS, 3 * LANES)
        for k in range(max(g * hz - 1, 0), g * hz + hz - 1):
            back_copy(k).start()

    send_back(0)
    if hy > 2:
        y_steps(hy - 2, near_parts)
    send_back(1)
    own_back = pltpu.make_async_copy(rs.at[0], rr.at[z], ld.at[6])
    own_back.start()
    for dist in range(hy - 2, 0, -1):
        if dist < hy - 2:
            y_steps(dist, near_parts)
        y_steps(dist, far_parts)
    weight_part(0)
    for parts_at in (near_parts, far_parts):
        for i in range(2):
            for side in (0, 1):
                y_copy(side, 1, parts_at[side][i]).wait_recv()
    total = ch[0] + (yl[0].astype(F32) + yr[0].astype(F32))
    gg_ref[...] = total[0:ff]
    gu_ref[...] = total[ff : 2 * ff]
    gd_ref[...] = total[2 * ff : 3 * ff]

    at = iota((toks, n), 1)
    block, row = lax.shift_right_logical(at, 4), at & (ROWS - 1)
    mine = block == ids_col
    take = hot(mine & (row == rank_col))
    take_0 = hot(mine & (row == rank_col + CAP) & (rank_col < SPARE))
    take_1 = hot(mine & (row == rank_col + CAP - SPARE) & (rank_col >= SPARE))
    take_high, take_low = hot(mine & (row == CAP)), hot(mine & (row == CAP + 1))

    for k in range(nz - 1):
        back_recv(k).wait_recv()
    own_back.wait()
    got = rr[...].reshape(n, 3 * LANES)
    tg_ref[:, 0 : 3 * LANES] = dot(take, got).astype(BF)
    tg_ref[:, 3 * LANES : 4 * LANES] = (
        dot(take_0, got[:, 0:LANES]) + dot(take_1, got[:, LANES : 2 * LANES])
    ).astype(BF)
    ends = got[:, 2 * LANES : 3 * LANES]
    chosen = iota((toks, LANES), 1) == rank_col
    value = jnp.where(chosen, dot(take_high, ends) + dot(take_low, ends), 0.0)
    value = jnp.sum(value, 1, keepdims=True) / probs_col
    pg_ref[...] = jnp.sum(jnp.where(eye, value, 0.0), 0, keepdims=True)

    for k in range(nz - 1):
        z_copies[k].wait_send()
        back_copy(k).wait_send()
    for p in range(nz):
        pass_right(p).wait_send()
        pass_left(p).wait_send()
        onward(p).wait_send()
    for copy in [mate_x, mate_d, mate_g] + prob_sends:
        copy.wait_send()
    for copy in tp_copies[0] + tp_copies[1]:
        copy.wait_send()
    for side in (0, 1):
        for part in far_parts[side]:
            y_copy(side, hy, part).wait_send()
        for dist in range(hy - 1, 0, -1):
            for part in range(4):
                y_copy(side, dist, part).wait_send()


def publish(*refs):
    copies = [pltpu.make_async_copy(refs[i], refs[i + 5], refs[10].at[i]) for i in range(5)]
    for copy in copies:
        copy.start()
    for copy in copies:
        copy.wait()


def shards(tokens, cotangent, expert_ids, gate_probs, w_gate, w_up, w_down):
    toks, width = tokens.shape
    ff = w_down.shape[1]
    nz, ny = lax.axis_size("ep"), lax.axis_size("island") // 2
    quarter, band = width // 4, width // (2 * ny)
    m = nz * CAP
    wide = quarter + LANES
    hy, hz = ny // 2, nz // 2
    hbm = pl.BlockSpec(memory_space=pltpu.HBM)
    vmem = pl.BlockSpec(memory_space=pltpu.VMEM)
    dma = pltpu.SemaphoreType.DMA
    shapes = (
        jax.ShapeDtypeStruct((toks, quarter), BF),
        jax.ShapeDtypeStruct((1, toks), F32),
        jax.ShapeDtypeStruct((ff, band), F32),
        jax.ShapeDtypeStruct((ff, band), F32),
        jax.ShapeDtypeStruct((ff, band), F32),
    )
    results = pl.pallas_call(
        functools.partial(kernel, nz, ny),
        out_shape=shapes,
        in_specs=[hbm, hbm, vmem, vmem, hbm, hbm, hbm],
        out_specs=(vmem,) * 5,
        scratch_shapes=[
            pltpu.VMEM((3 * ff, width), BF),
            pltpu.VMEM((toks, quarter), BF),
            pltpu.VMEM((toks, quarter), BF),
            pltpu.VMEM((nz, ROWS, wide), BF),
            pltpu.VMEM((4, nz, ROWS, wide), BF),
            pltpu.VMEM((ny, 2, m, band), BF),
            pltpu.VMEM((ny, 2, m, band), BF),
            pltpu.VMEM((ny, m, band), BF),
            pltpu.VMEM((ny, m, band), BF),
            pltpu.VMEM((3 * ff, m), BF),
            pltpu.VMEM((3 * ff, m), BF),
            pltpu.VMEM((ny, 3 * ff, band), F32),
            pltpu.VMEM((ny, 3 * ff, band), BF),
            pltpu.VMEM((hy, 3 * ff, band), BF),
            pltpu.VMEM((hy, 3 * ff, band), BF),
            pltpu.VMEM((4, m, quarter), BF),
            pltpu.VMEM((3, m, quarter), BF),
            pltpu.VMEM((4, nz, LANES), F32),
            pltpu.VMEM((nz, ROWS, 3 * LANES), BF),
            pltpu.VMEM((nz, ROWS, 3 * LANES), BF),
            dma((7,)),
            dma((nz,)), dma((nz,)),
            dma((3, nz)), dma((3, nz)),
            dma((3,)), dma((3,)),
            dma((4,)), dma((4,)),
            dma((2, 4)), dma((2, 4)),
            dma((2, hy + 1, 4)), dma((2, hy + 1, 4)),
            dma((nz,)), dma((nz,)),
        ],
        compiler_params=pltpu.CompilerParams(
            collective_id=0, has_side_effects=True, vmem_limit_bytes=(53 * 1024 + 384) * 1024
        ),
    )(
        tokens, cotangent,
        expert_ids.reshape(1, toks), gate_probs.reshape(1, toks),
        w_gate[0].T, w_up[0].T, w_down[0],
    )
    anywhere = pl.BlockSpec(memory_space=pl.ANY)
    token_grad, prob_grad, grad_gate, grad_up, grad_down = pl.pallas_call(
        publish,
        out_shape=shapes,
        in_specs=[anywhere] * 5,
        out_specs=(anywhere,) * 5,
        scratch_shapes=[dma((5,))],
        compiler_params=pltpu.CompilerParams(vmem_limit_bytes=4 * 1024 * 1024),
    )(*results)
    return (
        token_grad, prob_grad.reshape(toks, 1),
        grad_gate.T[None], grad_up.T[None], grad_down[None],
    )


def solution(mesh):
    rows = P(("island", "ep"), None)
    in_specs = (rows, rows, rows, rows, P("ep", None, "tp"), P("ep", None, "tp"), P("ep", "tp", None))
    out_specs = (
        P(("island", "ep"), "tp"), rows,
        P("ep", "island", "tp"), P("ep", "island", "tp"), P("ep", "tp", "island"),
    )
    return jax.shard_map(shards, mesh=mesh, in_specs=in_specs, out_specs=out_specs, check_vma=False)
```

profile of v0, /device:TPU:1, one launch (start us, length us, event | category | flops | bytes accessed | tf_op | source)
XLA Modules:
  0.0 73.3 jit_solution(10304917627665214685)
XLA Ops:
  0.6 0.0 copy-start
  0.6 0.0 copy-start.1
  0.7 0.6 copy-done
  1.3 0.0 copy-done.1
  1.3 71.2 %shard_map.110 = (bf16[128,512]{1,0:T(8,128)(2,1)S(1)}, f32[1,128]{1,0:T(1,128)S(1)}, f32[192,128]{1,0:T(8,128)S(1)}, f32[192,128]{1,0:T(8,128)S(1)}, f32[192,128]{1,0:T(8,128)S(1)}) custom-call(bf16[128,2048]{1,0:T(8,128)(2,1)} %tok.1, bf16[128,2048]{1,0:T(8,128)(2,1)} %cot.1, s32[1,128]{1,0:T(1,128)S(1)} %bitcast.17, f32[1,128]{1,0:T(1,128)S(1)} %bitcast.18, ...), custom_call_target="tpu_custom_call" | custom-call | tf_op jit(solution)/shard_map/pallas_call | solution.py:452
  72.5 0.8 %shard_map.111 = (bf16[128,512]{1,0:T(8,128)(2,1)}, f32[1,128]{1,0:T(1,128)}, f32[192,128]{1,0:T(8,128)}, f32[192,128]{1,0:T(8,128)}, f32[192,128]{1,0:T(8,128)}) custom-call(bf16[128,512]{1,0:T(8,128)(2,1)S(1)} %get-tuple-element.15.refs_0_, f32[1,128]{1,0:T(1,128)S(1)} %get-tuple-element.16.refs_1_, f32[192,128]{1,0:T(8,128)S(1)} %get-tuple-element.17.refs_2_, ...), custom_call_target="tpu_custom_call" | custom-call | tf_op jit(solution)/shard_map/pallas_call | solution.py:496
Async XLA Ops:
  0.6 0.7 copy-start
  0.6 0.7 copy-start.1
where the time goes:
time: 73.4 us; the launch traced here: 73.3 us
  Pallas kernels  72 us (98%)
    pallas_call x1, Pallas kernels, shards(): pl.pallas_call(functools.partial(kernel, nz, ny), out_shape=shapes, in_sp...  71.2 us

commit v1 on v0

--- a/solution.py
+++ b/solution.py
@@ -140,7 +140,8 @@
     z_copies = [z_copy(k) for k in range(nz - 1)]
     own_block = pltpu.make_async_copy(sb.at[z], rb.at[t, 0], ld.at[5])
     own_block.start()
-    for copy in z_copies:
+    ahead = 6
+    for copy in z_copies[:ahead]:
         copy.start()
 
     left_q, right_q, far_q = lax.rem(t + 3, 4), lax.rem(t + 1, 4), lax.rem(t + 2, 4)
@@ -179,6 +180,8 @@
             own_block.wait()
         else:
             z_copies[p - 1].wait_recv()
+            for copy in z_copies[p - 1 + ahead : p + ahead]:
+                copy.start()
         if p >= direct:
             onward(p).start()
         pass_right(p).start()
@@ -300,6 +303,19 @@
     for r in (2, 1, 3):
         tp_copies[1][r - 1].start()
 
+    input_part(0)
+    prob_row = jnp.sum(hidden.astype(F32) * back, 0, keepdims=True)
+    in_source = iota((nz, m), 0) == lax.shift_right_logical(iota((nz, m), 1) * 6554, 16)
+    at_row = iota((m, LANES), 0)
+    at_slot = iota((m, LANES), 1) == at_row - CAP * lax.shift_right_logical(at_row * 6554, 16)
+    pk[0] = dot(
+        jnp.where(in_source, prob_row, 0.0), jnp.where(at_slot, 1.0, 0.0),
+        precision=lax.Precision.HIGHEST,
+    )
+    prob_sends = [remote(pk.at[0], pk.at[r], ps.at[r], pr.at[r], tp_at(r)) for r in (1, 2, 3)]
+    for copy in prob_sends:
+        copy.start()
+
     mate_x.wait_recv()
     mate_d.wait_recv()
     mate_g.wait_recv()
@@ -307,22 +323,9 @@
     y_steps(hy, far_parts)
     weight_part(hy - 1, ny - hy + 1)
     y_steps(hy - 1, near_parts)
-
-    prob_row = jnp.sum(hidden.astype(F32) * back, 0, keepdims=True)
-    in_source = iota((nz, m), 0) == lax.shift_right_logical(iota((nz, m), 1) * 6554, 16)
-    at_row = iota((m, LANES), 0)
-    at_slot = iota((m, LANES), 1) == at_row - CAP * lax.shift_right_logical(at_row * 6554, 16)
-    pk[0] = dot(
-        jnp.where(in_source, prob_row, 0.0), jnp.where(at_slot, 1.0, 0.0),
-        precision=lax.Precision.HIGHEST,
-    )
-    prob_sends = [remote(pk.at[0], pk.at[r], ps.at[r], pr.at[r], tp_at(r)) for r in (1, 2, 3)]
-    for copy in prob_sends:
-        copy.start()
-    input_part(0)
+    if hy > 2:
+        weight_part(hy - 2, ny - hy + 2)
     y_steps(hy - 1, far_parts)
-    for dist in range(hy - 2, 0, -1):
-        weight_part(dist, ny - dist)
 
     for copy in prob_sends:
         copy.wait_recv()
@@ -363,15 +366,16 @@
             back_copy(k).start()
 
     send_back(0)
-    if hy > 2:
-        y_steps(hy - 2, near_parts)
-    send_back(1)
     own_back = pltpu.make_async_copy(rs.at[0], rr.at[z], ld.at[6])
     own_back.start()
     for dist in range(hy - 2, 0, -1):
-        if dist < hy - 2:
-            y_steps(dist, near_parts)
-        y_steps(dist, far_parts)
+        y_steps(dist, near_parts)
+        if dist > 1:
+            weight_part(dist - 1, ny - dist + 1)
+            y_steps(dist, far_parts)
+    send_back(1)
+    if hy > 2:
+        y_steps(1, far_parts)
     weight_part(0)
     for parts_at in (near_parts, far_parts):
         for i in range(2):

time: 73.4 us -> 75.8 us (1.033)
  the two profiles are of different devices: /device:TPU:1 before, /device:TPU:2 now
where the time goes in v1:
time: 75.8 us; the launch traced here: 75.6 us
  Pallas kernels  74.3 us (98%)
    pallas_call x1, Pallas kernels, shards(): pl.pallas_call(functools.partial(kernel, nz, ny), out_shape=shapes, in_sp...  73.5 us

profile of v1, /device:TPU:2, one launch (start us, length us, event | category | flops | bytes accessed | tf_op | source)
XLA Modules:
  0.0 75.6 jit_solution(12229970854166567450)
XLA Ops:
  0.6 0.0 copy-start
  0.6 0.0 copy-start.1
  0.7 0.6 copy-done
  1.3 0.0 copy-done.1
  1.3 73.5 %shard_map.110 = (bf16[128,512]{1,0:T(8,128)(2,1)S(1)}, f32[1,128]{1,0:T(1,128)S(1)}, f32[192,128]{1,0:T(8,128)S(1)}, f32[192,128]{1,0:T(8,128)S(1)}, f32[192,128]{1,0:T(8,128)S(1)}) custom-call(bf16[128,2048]{1,0:T(8,128)(2,1)} %tok.1, bf16[128,2048]{1,0:T(8,128)(2,1)} %cot.1, s32[1,128]{1,0:T(1,128)S(1)} %bitcast.17, f32[1,128]{1,0:T(1,128)S(1)} %bitcast.18, ...), custom_call_target="tpu_custom_call" | custom-call | tf_op jit(solution)/shard_map/pallas_call | solution.py:456
  74.8 0.8 %shard_map.111 = (bf16[128,512]{1,0:T(8,128)(2,1)}, f32[1,128]{1,0:T(1,128)}, f32[192,128]{1,0:T(8,128)}, f32[192,128]{1,0:T(8,128)}, f32[192,128]{1,0:T(8,128)}) custom-call(bf16[128,512]{1,0:T(8,128)(2,1)S(1)} %get-tuple-element.15.refs_0_, f32[1,128]{1,0:T(1,128)S(1)} %get-tuple-element.16.refs_1_, f32[192,128]{1,0:T(8,128)S(1)} %get-tuple-element.17.refs_2_, ...), custom_call_target="tpu_custom_call" | custom-call | tf_op jit(solution)/shard_map/pallas_call | solution.py:500
Async XLA Ops:
  0.6 0.7 copy-start
  0.6 0.7 copy-start.1

commit v2 on v1

--- a/solution.py
+++ b/solution.py
@@ -33,11 +33,7 @@
 
 
 def hops(nz):
-    near = [1, 2] if nz > 8 else []
-    pairs = []
-    for d in range(nz // 2 - 1, len(near), -1):
-        pairs += [d] + near[len(pairs) // 2 : len(pairs) // 2 + 1]
-    return [nz // 2] + [d for pair in pairs for d in (pair, nz - pair)]
+    return [d for near in range(1, nz // 2) for d in (near, nz - near)] + [nz // 2]
 
 
 def kernel(
@@ -140,8 +136,7 @@
     z_copies = [z_copy(k) for k in range(nz - 1)]
     own_block = pltpu.make_async_copy(sb.at[z], rb.at[t, 0], ld.at[5])
     own_block.start()
-    ahead = 6
-    for copy in z_copies[:ahead]:
+    for copy in reversed(z_copies):
         copy.start()
 
     left_q, right_q, far_q = lax.rem(t + 3, 4), lax.rem(t + 1, 4), lax.rem(t + 2, 4)
@@ -180,8 +175,6 @@
             own_block.wait()
         else:
             z_copies[p - 1].wait_recv()
-            for copy in z_copies[p - 1 + ahead : p + ahead]:
-                copy.start()
         if p >= direct:
             onward(p).start()
         pass_right(p).start()
@@ -299,9 +292,9 @@
 
     for r in (2, 1, 3):
         input_part(r)
+        tp_copies[1][r - 1].start()
+    for r in (2, 1, 3):
         tp_copies[0][r - 1].start()
-    for r in (2, 1, 3):
-        tp_copies[1][r - 1].start()
 
     input_part(0)
     prob_row = jnp.sum(hidden.astype(F32) * back, 0, keepdims=True)
@@ -362,18 +355,18 @@
         packed = dot(pack, summed[:, 0 : 3 * LANES])
         packed = packed + jnp.concatenate([dot(pack_0, ends), dot(pack_1, ends), extra], 1)
         rs[pl.ds(g * hz, hz)] = packed.astype(BF).reshape(hz, ROWS, 3 * LANES)
-        for k in range(max(g * hz - 1, 0), g * hz + hz - 1):
+        for k in reversed(range(max(g * hz - 1, 0), g * hz + hz - 1)):
             back_copy(k).start()
 
-    send_back(0)
-    own_back = pltpu.make_async_copy(rs.at[0], rr.at[z], ld.at[6])
-    own_back.start()
+    send_back(1)
     for dist in range(hy - 2, 0, -1):
         y_steps(dist, near_parts)
         if dist > 1:
             weight_part(dist - 1, ny - dist + 1)
             y_steps(dist, far_parts)
-    send_back(1)
+    send_back(0)
+    own_back = pltpu.make_async_copy(rs.at[0], rr.at[z], ld.at[6])
+    own_back.start()
     if hy > 2:
         y_steps(1, far_parts)
     weight_part(0)

time: 75.8 us -> 78 us (1.029)
  the two profiles are of different devices: /device:TPU:2 before, /device:TPU:1 now
where the time goes in v2:
time: 78 us; the launch traced here: 76.6 us
  Pallas kernels  75.3 us (97%)
    pallas_call x1, Pallas kernels, shards(): pl.pallas_call(functools.partial(kernel, nz, ny), out_shape=shapes, in_sp...  74.5 us

profile of v2, /device:TPU:1, one launch (start us, length us, event | category | flops | bytes accessed | tf_op | source)
XLA Modules:
  0.0 76.6 jit_solution(4345735130905507066)
XLA Ops:
  0.6 0.0 copy-start
  0.6 0.0 copy-start.1
  0.7 0.6 copy-done
  1.3 0.0 copy-done.1
  1.3 74.5 %shard_map.110 = (bf16[128,512]{1,0:T(8,128)(2,1)S(1)}, f32[1,128]{1,0:T(1,128)S(1)}, f32[192,128]{1,0:T(8,128)S(1)}, f32[192,128]{1,0:T(8,128)S(1)}, f32[192,128]{1,0:T(8,128)S(1)}) custom-call(bf16[128,2048]{1,0:T(8,128)(2,1)} %tok.1, bf16[128,2048]{1,0:T(8,128)(2,1)} %cot.1, s32[1,128]{1,0:T(1,128)S(1)} %bitcast.17, f32[1,128]{1,0:T(1,128)S(1)} %bitcast.18, ...), custom_call_target="tpu_custom_call" | custom-call | tf_op jit(solution)/shard_map/pallas_call | solution.py:449
  75.8 0.8 %shard_map.111 = (bf16[128,512]{1,0:T(8,128)(2,1)}, f32[1,128]{1,0:T(1,128)}, f32[192,128]{1,0:T(8,128)}, f32[192,128]{1,0:T(8,128)}, f32[192,128]{1,0:T(8,128)}) custom-call(bf16[128,512]{1,0:T(8,128)(2,1)S(1)} %get-tuple-element.15.refs_0_, f32[1,128]{1,0:T(1,128)S(1)} %get-tuple-element.16.refs_1_, f32[192,128]{1,0:T(8,128)S(1)} %get-tuple-element.17.refs_2_, ...), custom_call_target="tpu_custom_call" | custom-call | tf_op jit(solution)/shard_map/pallas_call | solution.py:493
Async XLA Ops:
  0.6 0.7 copy-start
  0.6 0.7 copy-start.1

commit v3 on v0

--- a/solution.py
+++ b/solution.py
@@ -321,8 +321,8 @@
         copy.start()
     input_part(0)
     y_steps(hy - 1, far_parts)
-    for dist in range(hy - 2, 0, -1):
-        weight_part(dist, ny - dist)
+    if hy > 2:
+        weight_part(hy - 2, ny - hy + 2)
 
     for copy in prob_sends:
         copy.wait_recv()
@@ -371,8 +371,23 @@
     for dist in range(hy - 2, 0, -1):
         if dist < hy - 2:
             y_steps(dist, near_parts)
+        else:
+            for at in range(dist - 1, 0, -1):
+                weight_part(at, ny - at)
         y_steps(dist, far_parts)
     weight_part(0)
+
+    for copy in z_copies + [mate_x, mate_d, mate_g] + prob_sends + tp_copies[0] + tp_copies[1]:
+        copy.wait_send()
+    for p in range(nz):
+        pass_right(p).wait_send()
+        pass_left(p).wait_send()
+        onward(p).wait_send()
+    for side in (0, 1):
+        for dist in range(hy, 1, -1):
+            for part in range(4):
+                if dist < hy or part in far_parts[side]:
+                    y_copy(side, dist, part).wait_send()
     for parts_at in (near_parts, far_parts):
         for i in range(2):
             for side in (0, 1):
@@ -405,22 +420,11 @@
     pg_ref[...] = jnp.sum(jnp.where(eye, value, 0.0), 0, keepdims=True)
 
     for k in range(nz - 1):
-        z_copies[k].wait_send()
         back_copy(k).wait_send()
-    for p in range(nz):
-        pass_right(p).wait_send()
-        pass_left(p).wait_send()
-        onward(p).wait_send()
-    for copy in [mate_x, mate_d, mate_g] + prob_sends:
-        copy.wait_send()
-    for copy in tp_copies[0] + tp_copies[1]:
-        copy.wait_send()
     for side in (0, 1):
-        for part in far_parts[side]:
-            y_copy(side, hy, part).wait_send()
-        for dist in range(hy - 1, 0, -1):
-            for part in range(4):
-                y_copy(side, dist, part).wait_send()
+        for part in range(4):
+            if hy > 1 or part in far_parts[side]:
+                y_copy(side, 1, part).wait_send()
 
 
 def publish(*refs):

time: 73.4 us -> 73.3 us (level)
  no operation moved by 1% of the time
where the time goes in v3:
time: 73.3 us; the launch traced here: 73.2 us
  Pallas kernels  71.8 us (98%)
    pallas_call x1, Pallas kernels, shards(): pl.pallas_call(functools.partial(kernel, nz, ny), out_shape=shapes, in_sp...  71 us

profile of v3, /device:TPU:1, one launch (start us, length us, event | category | flops | bytes accessed | tf_op | source)
XLA Modules:
  0.0 73.2 jit_solution(14455058438910257985)
XLA Ops:
  0.6 0.0 copy-start
  0.6 0.0 copy-start.1
  0.7 0.6 copy-done
  1.3 0.0 copy-done.1
  1.3 71.0 %shard_map.110 = (bf16[128,512]{1,0:T(8,128)(2,1)S(1)}, f32[1,128]{1,0:T(1,128)S(1)}, f32[192,128]{1,0:T(8,128)S(1)}, f32[192,128]{1,0:T(8,128)S(1)}, f32[192,128]{1,0:T(8,128)S(1)}) custom-call(bf16[128,2048]{1,0:T(8,128)(2,1)} %tok.1, bf16[128,2048]{1,0:T(8,128)(2,1)} %cot.1, s32[1,128]{1,0:T(1,128)S(1)} %bitcast.17, f32[1,128]{1,0:T(1,128)S(1)} %bitcast.18, ...), custom_call_target="tpu_custom_call" | custom-call | tf_op jit(solution)/shard_map/pallas_call | solution.py:456
  72.4 0.8 %shard_map.111 = (bf16[128,512]{1,0:T(8,128)(2,1)}, f32[1,128]{1,0:T(1,128)}, f32[192,128]{1,0:T(8,128)}, f32[192,128]{1,0:T(8,128)}, f32[192,128]{1,0:T(8,128)}) custom-call(bf16[128,512]{1,0:T(8,128)(2,1)S(1)} %get-tuple-element.15.refs_0_, f32[1,128]{1,0:T(1,128)S(1)} %get-tuple-element.16.refs_1_, f32[192,128]{1,0:T(8,128)S(1)} %get-tuple-element.17.refs_2_, ...), custom_call_target="tpu_custom_call" | custom-call | tf_op jit(solution)/shard_map/pallas_call | solution.py:500
Async XLA Ops:
  0.6 0.7 copy-start
  0.6 0.7 copy-start.1
